TPU v7x, 32 devices: a whole 2x2x4 slice. The times are simulated.
32 devices in a mesh: groups: 2 (over y), rows: 4 (over z), cols: 4 (over x, core).
Axes of the slice: x: 2, y: 2, z: 4, core: 2. Of those that a mesh axis runs over, the one named last changes fastest.
Arguments:
- positions: float32 [32, 4, 2, 1024], P(('groups', 'rows'), 'cols'), parts along dimension 0, may hold values from 0 to 1
- region_cell: int32 [32, 4], P(('groups', 'rows'), 'cols'), parts along dimension 0, may hold values from 0 to 63, as said below
- spread: float32 [32, 4, 1024], P(('groups', 'rows'), 'cols'), parts along dimension 0, may hold values from 0.4 to 0.8
- obs_var: float32 [32, 4, 1024], P(('groups', 'rows'), 'cols'), parts along dimension 0, may hold values from 1.05 to 1.6
- counts: int32 [32, 4], P(('groups', 'rows'), 'cols'), parts along dimension 0, may hold values from 1 to 1024, as said below
- pair_flags: int32 [32, 4, 16, 4], P(('groups', 'rows'), None, None, 'cols'), parts along dimension 0, may hold values from 0 to 1, as said below
- iterate: float32 [32, 4, 1024], P(('groups', 'rows'), 'cols'), parts along dimension 0, may hold values from -24 to 24
- residual: float32 [32, 4, 1024], P(('groups', 'rows'), 'cols'), parts along dimension 0, may hold values from -24 to 24
- direction: float32 [32, 4, 1024], P(('groups', 'rows'), 'cols'), parts along dimension 0, may hold values from -24 to 24
Outputs:
- iterate_next: float32 [32, 4, 1024], P(('groups', 'rows'), 'cols'), parts along dimension 0
- residual_next: float32 [32, 4, 1024], P(('groups', 'rows'), 'cols'), parts along dimension 0
- direction_next: float32 [32, 4, 1024], P(('groups', 'rows'), 'cols'), parts along dimension 0
There are 2 independent parts, one for each index of `groups`. A program takes and returns all parts, laid end to end along the dimension named above; each array names one. Nothing has to cross between parts.
Inputs may be any that keep to these rules, and one draw needn't show every extreme that they name: `counts`: each region holds 1 to 1024 observations; some region holds exactly 1024. `region_cell`: a permutation of the 64 cells of a grid of 16 rows by 4 columns. pair_flags[a, b] is 1 exactly where the cells of regions a and b differ by at most one in row and in column; the flags are symmetric; every region lists itself; no region lists more than 9 regions, itself included, and some list exactly 9.
All inputs are finite; a program needn't handle non-finite values.
Results may differ from a plain program's by a relative error of at most 0.00002.
Values sent between devices are 32-bit elements; how exact they have to be, the bound alone decides.
A program may use at most 64 MiB of HBM per device.

v0:
```python
import functools
import math

import jax
import jax.numpy as jnp
from jax import lax
from jax.experimental import pallas as pl
from jax.experimental.pallas import tpu as pltpu
from jax.sharding import PartitionSpec as P

ROOT_THREE = 1.7320508075688772
MATERN_LENGTH = 0.5
RATE = ROOT_THREE / MATERN_LENGTH
MESH = pl.DeviceIdType.MESH
LANES = 128
CHUNK = 32
BITS = RATE / math.log(2.0)
SCALE = 4.0 * RATE * BITS**-6 * 2.0**-BITS
TILE_COST, OWN_COST, PAIR_COST = 100, 130, 150
VMEM_BYTES = 40 * 1024 * 1024


def remote(src, dst, send_sem, recv_sem, device):
    return pltpu.make_async_remote_copy(
        src_ref=src,
        dst_ref=dst,
        send_sem=send_sem,
        recv_sem=recv_sem,
        device_id=device,
        device_id_type=MESH,
    )


def slot_numbers(shape):
    tile_at = lax.broadcasted_iota(jnp.int32, shape, 1)
    return tile_at * LANES + lax.broadcasted_iota(jnp.int32, shape, 2)


def gather_kernel(
    row_count, col_count, pos_ref, cell_ref, count_ref, spread_ref, dir_ref,
    row_out, col_out, meta_out, send_row, recv_row, send_col, recv_col, send_meta, recv_meta,
):
    my_row, my_col = lax.axis_index("rows"), lax.axis_index("cols")
    row_peers = [lax.rem(my_row + step, row_count) for step in range(1, row_count)]
    col_peers = [lax.rem(my_col + step, col_count) for step in range(1, col_count)]

    device_count = row_count * col_count
    me = my_row * col_count + my_col

    def place(peer):
        return {"rows": peer // col_count, "cols": peer % col_count}

    barrier = pltpu.get_barrier_semaphore()

    def greet(step, carry):
        peer = lax.rem(me + step, device_count)
        pl.semaphore_signal(barrier, inc=1, device_id=place(peer), device_id_type=MESH)
        return carry

    lax.fori_loop(1, device_count, greet, 0)
    local_rows, tiles, _ = spread_ref.shape
    cell = cell_ref[...].astype(jnp.float32)
    counts = count_ref[...]
    cell_row = jnp.floor((cell + 0.5) * (1.0 / col_count))
    cell_col = cell - cell_row * col_count
    live = slot_numbers((local_rows, tiles, LANES)) < counts.reshape(local_rows, 1, 1)
    weighted = spread_ref[...] * jnp.where(live, dir_ref[...], 0.0)
    line_at = lax.broadcasted_iota(jnp.int32, (local_rows, LANES), 0)
    lane_at = lax.broadcasted_iota(jnp.int32, (local_rows, LANES), 1)
    meta = jnp.where(
        lane_at == 2 * line_at,
        counts.astype(jnp.float32),
        jnp.where(lane_at == 2 * line_at + 1, cell, 0.0),
    )
    meta_out[me] = jnp.sum(meta, axis=0, keepdims=True).astype(jnp.int32)
    for axis, corner in enumerate((cell_row, cell_col)):
        for tile in range(tiles):
            line = pos_ref[:, axis, tile * LANES : (tile + 1) * LANES] + corner
            row_out[my_col, axis, :, tile, :] = line
            col_out[my_row, axis, :, tile, :] = line
    row_out[my_col, 2] = weighted
    col_out[my_row, 2] = weighted

    pl.semaphore_wait(barrier, device_count - 1)

    def send_metas(step, carry):
        peer = lax.rem(me + step, device_count)
        remote(
            meta_out.at[me], meta_out.at[me], send_meta.at[peer], recv_meta.at[me], place(peer)
        ).start()
        return carry

    def wait_metas(step, carry):
        peer = lax.rem(me + step, device_count)
        landed = remote(
            meta_out.at[me], meta_out.at[peer], send_meta.at[peer], recv_meta.at[peer], place(peer)
        )
        landed.wait_send()
        landed.wait_recv()
        return carry

    copies = []
    for peer in row_peers:
        copies.append((col_out, my_row, peer, send_row, recv_row, "rows"))
    for peer in col_peers:
        copies.append((row_out, my_col, peer, send_col, recv_col, "cols"))
    for ref, mine, peer, sends, recvs, axis in copies:
        remote(ref.at[mine], ref.at[mine], sends.at[peer], recvs.at[mine], {axis: peer}).start()
    lax.fori_loop(1, device_count, send_metas, 0)
    lax.fori_loop(1, device_count, wait_metas, 0)
    for ref, mine, peer, sends, recvs, axis in copies:
        landed = remote(ref.at[mine], ref.at[peer], sends.at[peer], recvs.at[peer], {axis: peer})
        landed.wait_send()
        landed.wait_recv()


def covariance(delta_x, delta_y):
    square = jnp.maximum(delta_x * delta_x + delta_y * delta_y, 1e-30)
    scaled = square * lax.rsqrt(square)
    gap = jnp.maximum(BITS - scaled, 0.0)
    power = jnp.exp2(gap)
    gap = gap * gap
    gap = gap * gap
    growth = (scaled + BITS / 4.0) * (scaled + BITS / RATE)
    return growth * gap * power


def tile_count(slots):
    return lax.shift_right_logical(slots + (LANES - 1), LANES.bit_length() - 1)


def choose_pairs(meta, cell_tiles, cell_row, cell_col, cell_line, load, chosen, sizes):
    row_count, col_count, local_rows = sizes
    grid_rows = row_count * local_rows
    my_row, my_col = lax.axis_index("rows"), lax.axis_index("cols")
    me = my_row * col_count + my_col

    def place_regions(row, carry):
        for col in range(col_count):
            device = row * col_count + col
            load[device] = 0
            for line in range(local_rows):
                cell = meta[device, 2 * line + 1]
                cell_tiles[cell] = tile_count(meta[device, 2 * line])
                cell_row[cell] = row
                cell_col[cell] = col
                cell_line[cell] = line
        return carry

    lax.fori_loop(0, row_count, place_regions, 0)
    for col in range(col_count):
        past = grid_rows * col_count + col
        cell_tiles[past] = 0
        cell_row[past] = 0
        cell_col[past] = 0
        cell_line[past] = 0

    def take(total, device, own_cell, other_cell, present):
        chosen[0, total] = own_cell
        chosen[1, total] = other_cell
        return total + jnp.where((device == me) & present, 1, 0)

    def cost(own_tiles, other_tiles):
        return own_tiles * (TILE_COST * other_tiles + OWN_COST) + PAIR_COST

    def same_cells(row, total):
        for col in range(col_count):
            cell = row * col_count + col
            tiles = cell_tiles[cell]
            device = cell_row[cell] * col_count + cell_col[cell]
            load[device] = load[device] + cost(tiles, tiles)
            total = take(total, device, cell, cell, True)
        return total

    def near_cells(row, total):
        for col in range(col_count):
            first = row * col_count + col
            first_tiles, first_row, first_col = cell_tiles[first], cell_row[first], cell_col[first]
            for down, across in ((0, 1), (1, -1), (1, 0), (1, 1)):
                if not 0 <= col + across < col_count:
                    continue
                second = first + down * col_count + across
                second_tiles = cell_tiles[second]
                second_row, second_col = cell_row[second], cell_col[second]
                forward = first_row * col_count + second_col
                backward = second_row * col_count + first_col
                forward_load = load[forward] + cost(first_tiles, second_tiles)
                backward_load = load[backward] + cost(second_tiles, first_tiles)
                ahead = forward_load <= backward_load
                present = second_tiles > 0
                device = jnp.where(ahead, forward, backward)
                load[device] = jnp.where(
                    present, jnp.where(ahead, forward_load, backward_load), load[device]
                )
                total = take(
                    total,
                    device,
                    jnp.where(ahead, first, second),
                    jnp.where(ahead, second, first),
                    present,
                )
        return total

    total = lax.fori_loop(0, grid_rows, same_cells, 0)
    return lax.fori_loop(0, grid_rows, near_cells, total)


def pair_kernel(
    meta, row_ref, col_ref, row_sum, col_sum, own_x, own_y, own_w, own_acc, other_acc,
    own_local, other_local, cell_tiles, cell_row, cell_col, cell_line, load, chosen,
):
    col_count, _, local_rows, _, _ = row_ref.shape
    row_count = col_ref.shape[0]
    row_sum[...] = jnp.zeros_like(row_sum)
    col_sum[...] = jnp.zeros_like(col_sum)
    total = choose_pairs(
        meta, cell_tiles, cell_row, cell_col, cell_line, load, chosen,
        (row_count, col_count, local_rows),
    )

    def skewed(line):
        wide = jnp.broadcast_to(line, (LANES, LANES))
        return pltpu.roll(wide, 0, 1, stride=1, stride_axis=0)

    def unskewed_sum(block):
        total = block[0:8]
        for start in range(8, LANES, 8):
            total = total + pltpu.roll(block[start : start + 8], LANES - start, 1)
        line_at = lax.broadcasted_iota(jnp.int32, (8, LANES), 0)
        for bit in (1, 2, 4):
            total = jnp.where((line_at & bit) != 0, pltpu.roll(total, LANES - bit, 1), total)
        return jnp.sum(total, axis=0, keepdims=True)

    def one_pair(index, carry):
        own_cell, other_cell = chosen[0, index], chosen[1, index]
        own_group, own_line = cell_col[own_cell], cell_line[own_cell]
        other_group, other_line = cell_row[other_cell], cell_line[other_cell]
        own_tiles, other_tiles = cell_tiles[own_cell], cell_tiles[other_cell]
        keep = jnp.where(own_cell == other_cell, 0.0, SCALE)
        for axis in range(2):
            origin = row_ref[own_group, axis, own_line, 0:1, 0:1]
            own_local[axis] = (row_ref[own_group, axis, own_line] - origin) * BITS
            other_local[axis] = (col_ref[other_group, axis, other_line] - origin) * BITS
        own_local[2] = row_ref[own_group, 2, own_line] * keep
        other_local[2] = col_ref[other_group, 2, other_line] * SCALE
        other_acc[...] = jnp.zeros_like(other_acc)

        def own_tile(tile, inner):
            here = pl.ds(tile, 1)
            own_x[...] = skewed(own_local[0, here, :])
            own_y[...] = skewed(own_local[1, here, :])
            own_w[...] = skewed(own_local[2, here, :])
            own_acc[...] = jnp.zeros_like(own_acc)

            def body(first, width):
                lines = [
                    [other_local[plane, pl.ds(first + step, 1), :] for plane in range(3)]
                    for step in range(width)
                ]
                totals = [other_acc[first + step] for step in range(width)]
                for start in range(0, LANES, CHUNK):
                    part = pl.ds(start, CHUNK)
                    part_x, part_y, part_w = own_x[part, :], own_y[part, :], own_w[part, :]
                    part_acc = own_acc[part, :]
                    for step in range(width):
                        line_x, line_y, line_w = lines[step]
                        value = covariance(part_x - line_x, part_y - line_y)
                        part_acc = part_acc + value * line_w
                        backward = value * part_w
                        totals[step] = totals[step] + jnp.sum(
                            backward.reshape(CHUNK // 8, 8, LANES), axis=0
                        )
                    own_acc[part, :] = part_acc
                for step in range(width):
                    other_acc[first + step] = totals[step]

            def two(pair, nested):
                body(pair * 2, 2)
                return nested

            lax.fori_loop(0, lax.shift_right_logical(other_tiles, 1), two, 0)

            @pl.when((other_tiles & 1) == 1)
            def _():
                body(other_tiles - 1, 1)

            row_sum[own_group, own_line, here, :] += unskewed_sum(own_acc[...])
            return inner

        lax.fori_loop(0, own_tiles, own_tile, 0)

        def finish(tile, inner):
            col_sum[other_group, other_line, pl.ds(tile, 1), :] += jnp.sum(
                other_acc[tile], axis=0, keepdims=True
            )
            return inner

        lax.fori_loop(0, other_tiles, finish, 0)
        return carry

    lax.fori_loop(0, total, one_pair, 0)


def step_kernel(
    row_count, col_count, row_sum, col_sum, spread_ref, var_ref, dir_ref, res_ref, iter_ref,
    count_ref, iter_out, res_out, dir_out, row_land, col_land, stats, mine_stats,
    send_row, recv_row, send_col, recv_col, send_stat, recv_stat,
):
    my_row, my_col = lax.axis_index("rows"), lax.axis_index("cols")
    device_count = row_count * col_count
    me = my_row * col_count + my_col
    row_peers = [lax.rem(my_row + step, row_count) for step in range(1, row_count)]
    col_peers = [lax.rem(my_col + step, col_count) for step in range(1, col_count)]

    def place(peer):
        return {"rows": peer // col_count, "cols": peer % col_count}

    barrier = pltpu.get_barrier_semaphore()

    def greet(step, carry):
        peer = lax.rem(me + step, device_count)
        pl.semaphore_signal(barrier, inc=1, device_id=place(peer), device_id_type=MESH)
        return carry

    lax.fori_loop(1, device_count, greet, 0)
    live = slot_numbers(spread_ref.shape) < count_ref[...]
    masked_dir = jnp.where(live, dir_ref[...], 0.0)
    masked_res = jnp.where(live, res_ref[...], 0.0)
    pl.semaphore_wait(barrier, device_count - 1)

    copies = []
    for peer in row_peers:
        copies.append((col_sum, col_land, my_row, peer, send_row, recv_row, "rows"))
    for peer in col_peers:
        copies.append((row_sum, row_land, my_col, peer, send_col, recv_col, "cols"))
    for src, dst, mine, peer, sends, recvs, axis in copies:
        remote(src.at[peer], dst.at[mine], sends.at[peer], recvs.at[mine], {axis: peer}).start()
    total = row_sum[my_col] + col_sum[my_row]
    for src, dst, mine, peer, sends, recvs, axis in copies:
        landed = remote(src.at[peer], dst.at[peer], sends.at[peer], recvs.at[peer], {axis: peer})
        landed.wait_send()
        landed.wait_recv()
        total = total + dst[peer]

    image = jnp.where(live, spread_ref[...] * total + var_ref[...] * masked_dir, 0.0)

    def lane_sum(values):
        return jnp.sum(jnp.sum(values, axis=0), axis=0, keepdims=True)

    for index, values in enumerate(
        (masked_res * masked_res, masked_dir * image, masked_res * image, image * image)
    ):
        mine_stats[pl.ds(index, 1), :] = lane_sum(values)
    stats[me] = mine_stats[...]

    def send_stats(step, carry):
        peer = lax.rem(me + step, device_count)
        remote(
            mine_stats, stats.at[me], send_stat.at[peer], recv_stat.at[me], place(peer)
        ).start()
        return carry

    def wait_stats(step, carry):
        peer = lax.rem(me + step, device_count)
        landed = remote(
            mine_stats, stats.at[peer], send_stat.at[peer], recv_stat.at[peer], place(peer)
        )
        landed.wait_send()
        landed.wait_recv()
        return carry

    lax.fori_loop(1, device_count, send_stats, 0)
    lax.fori_loop(1, device_count, wait_stats, 0)
    sums = jnp.sum(jnp.sum(stats[...], axis=0), axis=1, keepdims=True)
    res_norm, curvature, cross, image_norm = (sums[at : at + 1, :][None] for at in range(4))
    step_size = res_norm / curvature
    next_norm = res_norm - 2.0 * step_size * cross + step_size * step_size * image_norm
    residual_next = masked_res - step_size * image
    iter_out[...] = jnp.where(live, iter_ref[...], 0.0) + step_size * masked_dir
    res_out[...] = residual_next
    dir_out[...] = residual_next + next_norm / res_norm * masked_dir


def vmem(count):
    return [pl.BlockSpec(memory_space=pltpu.VMEM)] * count


def local(
    row_count, col_count, positions, region_cell, spread, obs_var, counts, pair_flags, iterate,
    residual, direction,
):
    local_rows, _, slots = spread.shape
    tiles = slots // LANES
    flat = (local_rows, tiles, LANES)
    device_count = row_count * col_count
    f32, i32 = jnp.float32, jnp.int32
    dma = pltpu.SemaphoreType.DMA
    spread_l, var_l, iter_l, res_l, dir_l = (
        value.reshape(flat) for value in (spread, obs_var, iterate, residual, direction)
    )
    grid_cells = device_count * local_rows
    row_part, col_part, meta = pl.pallas_call(
        functools.partial(gather_kernel, row_count, col_count),
        out_shape=(
            jax.ShapeDtypeStruct((col_count, 3, local_rows, tiles, LANES), f32),
            jax.ShapeDtypeStruct((row_count, 3, local_rows, tiles, LANES), f32),
            jax.ShapeDtypeStruct((device_count, 1, LANES), i32),
        ),
        in_specs=vmem(5),
        out_specs=tuple(vmem(3)),
        scratch_shapes=[
            dma((row_count,)),
            dma((row_count,)),
            dma((col_count,)),
            dma((col_count,)),
            dma((device_count,)),
            dma((device_count,)),
        ],
        compiler_params=pltpu.CompilerParams(
            collective_id=0, has_side_effects=True, vmem_limit_bytes=VMEM_BYTES
        ),
        name="gather_parts",
    )(positions.reshape(local_rows, 2, slots), region_cell, counts, spread_l, dir_l)

    row_sum, col_sum = pl.pallas_call(
        pair_kernel,
        out_shape=(
            jax.ShapeDtypeStruct((col_count, local_rows, tiles, LANES), f32),
            jax.ShapeDtypeStruct((row_count, local_rows, tiles, LANES), f32),
        ),
        in_specs=[pl.BlockSpec(memory_space=pltpu.SMEM)] + vmem(2),
        out_specs=tuple(vmem(2)),
        scratch_shapes=[pltpu.VMEM((LANES, LANES), f32)] * 4
        + [
            pltpu.VMEM((tiles, 8, LANES), f32),
            pltpu.VMEM((3, tiles, LANES), f32),
            pltpu.VMEM((3, tiles, LANES), f32),
        ]
        + [pltpu.SMEM((grid_cells + col_count,), i32)] * 4
        + [pltpu.SMEM((device_count,), i32), pltpu.SMEM((2, 5 * grid_cells + 1), i32)],
        compiler_params=pltpu.CompilerParams(vmem_limit_bytes=VMEM_BYTES),
        name="pair_sums",
    )(meta.reshape(device_count, LANES), row_part, col_part)

    outs = pl.pallas_call(
        functools.partial(step_kernel, row_count, col_count),
        out_shape=(jax.ShapeDtypeStruct(flat, f32),) * 3,
        in_specs=vmem(8),
        out_specs=tuple(vmem(3)),
        scratch_shapes=[
            pltpu.VMEM((col_count, local_rows, tiles, LANES), f32),
            pltpu.VMEM((row_count, local_rows, tiles, LANES), f32),
            pltpu.VMEM((device_count, 4, LANES), f32),
            pltpu.VMEM((4, LANES), f32),
            dma((row_count,)),
            dma((row_count,)),
            dma((col_count,)),
            dma((col_count,)),
            dma((device_count,)),
            dma((device_count,)),
        ],
        compiler_params=pltpu.CompilerParams(
            collective_id=1, has_side_effects=True, vmem_limit_bytes=VMEM_BYTES
        ),
        name="reduce_and_step",
    )(row_sum, col_sum, spread_l, var_l, dir_l, res_l, iter_l, counts.reshape(local_rows, 1, 1))
    return tuple(out.reshape(spread.shape) for out in outs)


def solution(mesh):
    per_slot = P(("groups", "rows"), "cols", None)
    return jax.shard_map(
        functools.partial(local, mesh.shape["rows"], mesh.shape["cols"]),
        mesh=mesh,
        in_specs=(
            P(("groups", "rows"), "cols", None, None),
            P(("groups", "rows"), "cols"),
            per_slot,
            per_slot,
            P(("groups", "rows"), "cols"),
            P(("groups", "rows"), None, None, "cols"),
            per_slot,
            per_slot,
            per_slot,
        ),
        out_specs=(per_slot, per_slot, per_slot),
        check_vma=False,
    )
```

profile of v0, /device:TPU:0, one launch (start us, length us, event | category | flops | bytes accessed | tf_op | source)
XLA Modules:
  0.0 72.5 jit_solution(1683998264394938940)
XLA Ops:
  0.6 0.0 copy-start.9
  0.6 0.6 copy-done.9
  1.3 0.1 copy.11.cell_ref
  1.4 0.6 copy-done.8
  1.9 0.1 copy.12.count_ref
  2.0 0.7 copy-done
  2.8 0.7 copy-done.2
  3.5 0.8 %copy-done.4 = f32[4,1,2,1024]{3,2,1,0:T(2,128)S(1)} copy-done((f32[4,1,2,1024]{3,2,1,0:T(2,128)S(1)}, f32[4,1,2,1024]{3,2,1,0:T(2,128)}, u32[]{:S(2)}) %copy-start.4) | copy-done | bytes 32792
  4.2 12.4 %gather_parts.1 = (f32[4,3,4,8,128]{4,3,2,1,0:T(8,128)S(1)}, f32[4,3,4,8,128]{4,3,2,1,0:T(8,128)S(1)}, s32[16,1,128]{2,1,0:T(1,128)S(1)}) custom-call(f32[4,2,1024]{2,1,0:T(2,128)S(1)} %bitcast.15, s32[4,1]{1,0:T(4,128)S(1)} %copy.11.cell_ref, s32[4,1]{1,0:T(4,128)S(1)} %copy.12.count_ref, f32[4,8,128]{2,1,0:T(8,128)S(1)} %bitcast.11, f32[4,8,128]{2,1,0:T(8,128)S(1)} %bitcast.13), custom_call_target="tpu_custom_call" | custom-call | tf_op jit(solution)/shard_map/gather_parts/pallas_call | solution.py:402
  16.6 0.0 copy-start.1
  16.6 0.0 copy-start.3
  16.6 0.0 copy-start.5
  16.6 0.0 copy-start.6
  16.6 0.0 copy-start.7
  16.7 41.4 %pair_sums.1 = (f32[4,4,8,128]{3,2,1,0:T(8,128)S(1)}, f32[4,4,8,128]{3,2,1,0:T(8,128)S(1)}) custom-call(s32[16,128]{1,0:T(8,128)S(1)} %bitcast.22, f32[4,3,4,8,128]{4,3,2,1,0:T(8,128)S(1)} %get-tuple-element.12.row_ref, f32[4,3,4,8,128]{4,3,2,1,0:T(8,128)S(1)} %get-tuple-element.13.col_ref), custom_call_target="tpu_custom_call" | custom-call | tf_op jit(solution)/shard_map/pair_sums/pallas_call | solution.py:425
  58.0 0.1 copy.13.count_ref
  58.1 0.0 copy-done.1
  58.1 0.0 copy-done.3
  58.1 0.0 copy-done.5
  58.1 0.0 copy-done.6
  58.1 12.6 %reduce_and_step.1 = (f32[4,8,128]{2,1,0:T(8,128)S(1)}, f32[4,8,128]{2,1,0:T(8,128)S(1)}, f32[4,8,128]{2,1,0:T(8,128)S(1)}) custom-call(f32[4,4,8,128]{3,2,1,0:T(8,128)S(1)} %get-tuple-element.14.row_sum, f32[4,4,8,128]{3,2,1,0:T(8,128)S(1)} %get-tuple-element.15.col_sum, f32[4,8,128]{2,1,0:T(8,128)S(1)} %bitcast.12, f32[4,8,128]{2,1,0:T(8,128)S(1)} %bitcast.19, ...), custom_call_target="tpu_custom_call" | custom-call | tf_op jit(solution)/shard_map/reduce_and_step/pallas_call | solution.py:445
  70.7 0.6 copy.20
  71.3 0.6 copy.21
  71.9 0.6 copy.22
  (5 shorter events, 0.0 us)
Async XLA Ops:
  0.6 0.7 copy-start.9
  1.3 0.7 copy-start.8
  2.0 0.7 copy-start
  2.8 0.7 copy-start.2
  3.5 0.8 %copy-start.4 = (f32[4,1,2,1024]{3,2,1,0:T(2,128)S(1)}, f32[4,1,2,1024]{3,2,1,0:T(2,128)}, u32[]{:S(2)}) copy-start(f32[4,1,2,1024]{3,2,1,0:T(2,128)} %param.9) | copy-start | bytes 98308
  16.6 41.5 %copy-start.1 = (f32[4,1,1024]{2,1,0:T(1,128)S(1)}, f32[4,1,1024]{2,1,0:T(1,128)}, u32[]{:S(2)}) copy-start(f32[4,1,1024]{2,1,0:T(1,128)} %param.11) | copy-start | bytes 49156
  16.6 41.5 %copy-start.3 = (f32[4,1,1024]{2,1,0:T(1,128)S(1)}, f32[4,1,1024]{2,1,0:T(1,128)}, u32[]{:S(2)}) copy-start(f32[4,1,1024]{2,1,0:T(1,128)} %param.16) | copy-start | bytes 49156
  16.6 41.5 %copy-start.5 = (f32[4,1,1024]{2,1,0:T(1,128)S(1)}, f32[4,1,1024]{2,1,0:T(1,128)}, u32[]{:S(2)}) copy-start(f32[4,1,1024]{2,1,0:T(1,128)} %param.12) | copy-start | bytes 49156
  16.6 41.5 %copy-start.6 = (f32[4,1,1024]{2,1,0:T(1,128)S(1)}, f32[4,1,1024]{2,1,0:T(1,128)}, u32[]{:S(2)}) copy-start(f32[4,1,1024]{2,1,0:T(1,128)} %param.15) | copy-start | bytes 49156
  16.6 41.5 %copy-start.7 = (f32[4,1,1024]{2,1,0:T(1,128)S(1)}, f32[4,1,1024]{2,1,0:T(1,128)}, u32[]{:S(2)}) copy-start(f32[4,1,1024]{2,1,0:T(1,128)} %param.14) | copy-start | bytes 49156
where the time goes:
time: 71.6 us; the launch traced here: 72.5 us
  Pallas kernels  66.3 us (93%)
  local copies, waits for them, and re-layouts  5.53 us (8%)
  between operations  0.72 us (1%)
    pallas_call x1, Pallas kernels, local(): pl.pallas_call(pair_kernel, out_shape=(jax.ShapeDtypeStruct((col_count, l...  41.4 us
    pallas_call x1, Pallas kernels, local(): pl.pallas_call(functools.partial(step_kernel, row_count, col_count), out_...  12.6 us
    pallas_call x1, Pallas kernels, local(): pl.pallas_call(functools.partial(gather_kernel, row_count, col_count), ou...  12.4 us
    unnamed x25, local copies, waits for them, and re-layouts  5.43 us

commit v1 on v0

--- a/solution.py
+++ b/solution.py
@@ -14,6 +14,7 @@
 MESH = pl.DeviceIdType.MESH
 LANES = 128
 CHUNK = 32
+GROUP = 2
 BITS = RATE / math.log(2.0)
 SCALE = 4.0 * RATE * BITS**-6 * 2.0**-BITS
 TILE_COST, OWN_COST, PAIR_COST = 100, 130, 150
@@ -161,7 +162,8 @@
         return total + jnp.where((device == me) & present, 1, 0)
 
     def cost(own_tiles, other_tiles):
-        return own_tiles * (TILE_COST * other_tiles + OWN_COST) + PAIR_COST
+        least = jnp.minimum(own_tiles, other_tiles)
+        return TILE_COST * own_tiles * other_tiles + OWN_COST * least + PAIR_COST
 
     def same_cells(row, total):
         for col in range(col_count):
@@ -184,13 +186,13 @@
                 second_row, second_col = cell_row[second], cell_col[second]
                 forward = first_row * col_count + second_col
                 backward = second_row * col_count + first_col
-                forward_load = load[forward] + cost(first_tiles, second_tiles)
-                backward_load = load[backward] + cost(second_tiles, first_tiles)
+                work = cost(first_tiles, second_tiles)
+                forward_load, backward_load = load[forward], load[backward]
                 ahead = forward_load <= backward_load
                 present = second_tiles > 0
                 device = jnp.where(ahead, forward, backward)
-                load[device] = jnp.where(
-                    present, jnp.where(ahead, forward_load, backward_load), load[device]
+                load[device] = jnp.minimum(forward_load, backward_load) + jnp.where(
+                    present, work, 0
                 )
                 total = take(
                     total,
@@ -206,8 +208,8 @@
 
 
 def pair_kernel(
-    meta, row_ref, col_ref, row_sum, col_sum, own_x, own_y, own_w, own_acc, other_acc,
-    own_local, other_local, cell_tiles, cell_row, cell_col, cell_line, load, chosen,
+    meta, row_ref, col_ref, row_sum, col_sum, own_wide, own_acc, other_acc,
+    own_local, other_local, sums, cell_tiles, cell_row, cell_col, cell_line, load, chosen,
 ):
     col_count, _, local_rows, _, _ = row_ref.shape
     row_count = col_ref.shape[0]
@@ -218,41 +220,42 @@
         (row_count, col_count, local_rows),
     )
 
-    def skewed(line):
-        wide = jnp.broadcast_to(line, (LANES, LANES))
-        return pltpu.roll(wide, 0, 1, stride=1, stride_axis=0)
-
-    def unskewed_sum(block):
-        total = block[0:8]
-        for start in range(8, LANES, 8):
-            total = total + pltpu.roll(block[start : start + 8], LANES - start, 1)
-        line_at = lax.broadcasted_iota(jnp.int32, (8, LANES), 0)
-        for bit in (1, 2, 4):
-            total = jnp.where((line_at & bit) != 0, pltpu.roll(total, LANES - bit, 1), total)
-        return jnp.sum(total, axis=0, keepdims=True)
-
     def one_pair(index, carry):
-        own_cell, other_cell = chosen[0, index], chosen[1, index]
-        own_group, own_line = cell_col[own_cell], cell_line[own_cell]
-        other_group, other_line = cell_row[other_cell], cell_line[other_cell]
-        own_tiles, other_tiles = cell_tiles[own_cell], cell_tiles[other_cell]
-        keep = jnp.where(own_cell == other_cell, 0.0, SCALE)
+        row_cell, col_cell = chosen[0, index], chosen[1, index]
+        row_group, row_line = cell_col[row_cell], cell_line[row_cell]
+        col_group, col_line = cell_row[col_cell], cell_line[col_cell]
+        row_tiles, col_tiles = cell_tiles[row_cell], cell_tiles[col_cell]
+        swap = col_tiles < row_tiles
+        own_tiles = jnp.minimum(row_tiles, col_tiles)
+        other_tiles = jnp.maximum(row_tiles, col_tiles)
+        keep = jnp.where(row_cell == col_cell, 0.0, SCALE)
         for axis in range(2):
-            origin = row_ref[own_group, axis, own_line, 0:1, 0:1]
-            own_local[axis] = (row_ref[own_group, axis, own_line] - origin) * BITS
-            other_local[axis] = (col_ref[other_group, axis, other_line] - origin) * BITS
-        own_local[2] = row_ref[own_group, 2, own_line] * keep
-        other_local[2] = col_ref[other_group, 2, other_line] * SCALE
+            origin = row_ref[row_group, axis, row_line, 0:1, 0:1]
+            row_axis = (row_ref[row_group, axis, row_line] - origin) * BITS
+            col_axis = (col_ref[col_group, axis, col_line] - origin) * BITS
+            own_local[axis] = jnp.where(swap, col_axis, row_axis)
+            other_local[axis] = jnp.where(swap, row_axis, col_axis)
+        row_weight = row_ref[row_group, 2, row_line] * keep
+        col_weight = col_ref[col_group, 2, col_line] * SCALE
+        own_local[2] = jnp.where(swap, col_weight, row_weight)
+        other_local[2] = jnp.where(swap, row_weight, col_weight)
         other_acc[...] = jnp.zeros_like(other_acc)
+        sums[...] = jnp.zeros_like(sums)
+
+        def spread_out(group, inner):
+            for step in range(GROUP):
+                tile = group * GROUP + step
+                here = pl.ds(tile, 1)
+                for plane in range(3):
+                    line = jnp.broadcast_to(own_local[plane, here, :], (LANES, LANES))
+                    own_wide[tile, plane] = line.T
+            return inner
+
+        groups = lax.shift_right_logical(own_tiles + (GROUP - 1), GROUP.bit_length() - 1)
+        lax.fori_loop(0, groups, spread_out, 0)
 
         def own_tile(tile, inner):
-            here = pl.ds(tile, 1)
-            own_x[...] = skewed(own_local[0, here, :])
-            own_y[...] = skewed(own_local[1, here, :])
-            own_w[...] = skewed(own_local[2, here, :])
-            own_acc[...] = jnp.zeros_like(own_acc)
-
-            def body(first, width):
+            def body(first, width, fresh):
                 lines = [
                     [other_local[plane, pl.ds(first + step, 1), :] for plane in range(3)]
                     for step in range(width)
@@ -260,8 +263,8 @@
                 totals = [other_acc[first + step] for step in range(width)]
                 for start in range(0, LANES, CHUNK):
                     part = pl.ds(start, CHUNK)
-                    part_x, part_y, part_w = own_x[part, :], own_y[part, :], own_w[part, :]
-                    part_acc = own_acc[part, :]
+                    part_x, part_y, part_w = (own_wide[tile, plane, part, :] for plane in range(3))
+                    part_acc = 0.0 if fresh else own_acc[tile, part, :]
                     for step in range(width):
                         line_x, line_y, line_w = lines[step]
                         value = covariance(part_x - line_x, part_y - line_y)
@@ -270,32 +273,44 @@
                         totals[step] = totals[step] + jnp.sum(
                             backward.reshape(CHUNK // 8, 8, LANES), axis=0
                         )
-                    own_acc[part, :] = part_acc
+                    own_acc[tile, part, :] = part_acc
                 for step in range(width):
                     other_acc[first + step] = totals[step]
 
+            odd = other_tiles & 1
+
+            @pl.when(odd == 1)
+            def _():
+                body(0, 1, True)
+
+            @pl.when(odd == 0)
+            def _():
+                body(0, 2, True)
+
             def two(pair, nested):
-                body(pair * 2, 2)
+                body(pair * 2 + odd, 2, False)
                 return nested
 
-            lax.fori_loop(0, lax.shift_right_logical(other_tiles, 1), two, 0)
-
-            @pl.when((other_tiles & 1) == 1)
-            def _():
-                body(other_tiles - 1, 1)
-
-            row_sum[own_group, own_line, here, :] += unskewed_sum(own_acc[...])
+            lax.fori_loop(1 - odd, lax.shift_right_logical(other_tiles, 1), two, 0)
             return inner
 
         lax.fori_loop(0, own_tiles, own_tile, 0)
 
-        def finish(tile, inner):
-            col_sum[other_group, other_line, pl.ds(tile, 1), :] += jnp.sum(
-                other_acc[tile], axis=0, keepdims=True
-            )
+        def own_finish(group, inner):
+            for step in range(GROUP):
+                tile = group * GROUP + step
+                sums[0, pl.ds(tile, 1), :] = jnp.sum(own_acc[tile].T, axis=0, keepdims=True)
             return inner
 
-        lax.fori_loop(0, other_tiles, finish, 0)
+        lax.fori_loop(0, groups, own_finish, 0)
+
+        def other_finish(tile, inner):
+            sums[1, pl.ds(tile, 1), :] = jnp.sum(other_acc[tile], axis=0, keepdims=True)
+            return inner
+
+        lax.fori_loop(0, other_tiles, other_finish, 0)
+        row_sum[row_group, row_line] += jnp.where(swap, sums[1], sums[0])
+        col_sum[col_group, col_line] += jnp.where(swap, sums[0], sums[1])
         return carry
 
     lax.fori_loop(0, total, one_pair, 0)
@@ -430,11 +445,13 @@
         ),
         in_specs=[pl.BlockSpec(memory_space=pltpu.SMEM)] + vmem(2),
         out_specs=tuple(vmem(2)),
-        scratch_shapes=[pltpu.VMEM((LANES, LANES), f32)] * 4
-        + [
+        scratch_shapes=[
+            pltpu.VMEM((tiles, 3, LANES, LANES), f32),
+            pltpu.VMEM((tiles, LANES, LANES), f32),
             pltpu.VMEM((tiles, 8, LANES), f32),
             pltpu.VMEM((3, tiles, LANES), f32),
             pltpu.VMEM((3, tiles, LANES), f32),
+            pltpu.VMEM((2, tiles, LANES), f32),
         ]
         + [pltpu.SMEM((grid_cells + col_count,), i32)] * 4
         + [pltpu.SMEM((device_count,), i32), pltpu.SMEM((2, 5 * grid_cells + 1), i32)],

time: 71.6 us -> 54.8 us (0.77)
  Pallas kernels: 66.3 us -> 48.8 us
    pallas_call x1, Pallas kernels: 41.4 us -> 20.6 us  [local(): pl.pallas_call(pair_kernel, out_shape=(jax.ShapeDtypeStruct((col_count, l...]
    pallas_call x1, Pallas kernels: 12.6 us -> 15.8 us  [local(): pl.pallas_call(functools.partial(step_kernel, row_count, col_count), out_...]
where the time goes in v1:
time: 54.8 us; the launch traced here: 55 us
  Pallas kernels  48.8 us (89%)
  local copies, waits for them, and re-layouts  5.53 us (10%)
  between operations  0.72 us (1%)
    pallas_call x1, Pallas kernels, local(): pl.pallas_call(pair_kernel, out_shape=(jax.ShapeDtypeStruct((col_count, l...  20.6 us
    pallas_call x1, Pallas kernels, local(): pl.pallas_call(functools.partial(step_kernel, row_count, col_count), out_...  15.8 us
    pallas_call x1, Pallas kernels, local(): pl.pallas_call(functools.partial(gather_kernel, row_count, col_count), ou...  12.4 us
    unnamed x25, local copies, waits for them, and re-layouts  5.43 us

profile of v1, /device:TPU:0, one launch (start us, length us, event | category | flops | bytes accessed | tf_op | source)
XLA Modules:
  0.0 55.0 jit_solution(11722419236278176667)
XLA Ops:
  0.6 0.0 copy-start.9
  0.6 0.6 %copy-done.9 = s32[4,1]{0,1:T(1,128)S(1)} copy-done((s32[4,1]{0,1:T(1,128)S(1)}, s32[4,1]{0,1:T(1,128)}, u32[]{:S(2)}) %copy-start.9) | copy-done | bytes 40
  1.3 0.1 copy.11.cell_ref
  1.4 0.6 %copy-done.8 = s32[4,1]{0,1:T(1,128)S(1)} copy-done((s32[4,1]{0,1:T(1,128)S(1)}, s32[4,1]{0,1:T(1,128)}, u32[]{:S(2)}) %copy-start.8) | copy-done | bytes 40
  1.9 0.1 copy.12.count_ref
  2.0 0.7 %copy-done = f32[4,1,1024]{2,1,0:T(1,128)S(1)} copy-done((f32[4,1,1024]{2,1,0:T(1,128)S(1)}, f32[4,1,1024]{2,1,0:T(1,128)}, u32[]{:S(2)}) %copy-start) | copy-done | bytes 16408
  2.8 0.7 %copy-done.2 = f32[4,1,1024]{2,1,0:T(1,128)S(1)} copy-done((f32[4,1,1024]{2,1,0:T(1,128)S(1)}, f32[4,1,1024]{2,1,0:T(1,128)}, u32[]{:S(2)}) %copy-start.2) | copy-done | bytes 16408
  3.5 0.8 %copy-done.4 = f32[4,1,2,1024]{3,2,1,0:T(2,128)S(1)} copy-done((f32[4,1,2,1024]{3,2,1,0:T(2,128)S(1)}, f32[4,1,2,1024]{3,2,1,0:T(2,128)}, u32[]{:S(2)}) %copy-start.4) | copy-done | bytes 32792
  4.2 12.4 %gather_parts.1 = (f32[4,3,4,8,128]{4,3,2,1,0:T(8,128)S(1)}, f32[4,3,4,8,128]{4,3,2,1,0:T(8,128)S(1)}, s32[16,1,128]{2,1,0:T(1,128)S(1)}) custom-call(f32[4,2,1024]{2,1,0:T(2,128)S(1)} %bitcast.15, s32[4,1]{1,0:T(4,128)S(1)} %copy.11.cell_ref, s32[4,1]{1,0:T(4,128)S(1)} %copy.12.count_ref, f32[4,8,128]{2,1,0:T(8,128)S(1)} %bitcast.11, f32[4,8,128]{2,1,0:T(8,128)S(1)} %bitcast.13), custom_call_target="tpu_custom_call" | custom-call | tf_op jit(solution)/shard_map/gather_parts/pallas_call | solution.py:417
  16.6 0.0 copy-start.1
  16.6 0.0 copy-start.3
  16.6 0.0 copy-start.5
  16.6 0.0 copy-start.6
  16.6 0.0 copy-start.7
  16.7 20.6 %pair_sums.1 = (f32[4,4,8,128]{3,2,1,0:T(8,128)S(1)}, f32[4,4,8,128]{3,2,1,0:T(8,128)S(1)}) custom-call(s32[16,128]{1,0:T(8,128)S(1)} %bitcast.22, f32[4,3,4,8,128]{4,3,2,1,0:T(8,128)S(1)} %get-tuple-element.12.row_ref, f32[4,3,4,8,128]{4,3,2,1,0:T(8,128)S(1)} %get-tuple-element.13.col_ref), custom_call_target="tpu_custom_call" | custom-call | tf_op jit(solution)/shard_map/pair_sums/pallas_call | solution.py:440
  37.3 0.1 copy.13.count_ref
  37.4 0.0 copy-done.1
  37.4 0.0 copy-done.3
  37.4 0.0 copy-done.5
  37.4 0.0 copy-done.6
  37.4 15.8 %reduce_and_step.1 = (f32[4,8,128]{2,1,0:T(8,128)S(1)}, f32[4,8,128]{2,1,0:T(8,128)S(1)}, f32[4,8,128]{2,1,0:T(8,128)S(1)}) custom-call(f32[4,4,8,128]{3,2,1,0:T(8,128)S(1)} %get-tuple-element.14.row_sum, f32[4,4,8,128]{3,2,1,0:T(8,128)S(1)} %get-tuple-element.15.col_sum, f32[4,8,128]{2,1,0:T(8,128)S(1)} %bitcast.12, f32[4,8,128]{2,1,0:T(8,128)S(1)} %bitcast.19, ...), custom_call_target="tpu_custom_call" | custom-call | tf_op jit(solution)/shard_map/reduce_and_step/pallas_call | solution.py:462
  53.2 0.6 %copy.20 = f32[4,1,1024]{2,1,0:T(1,128)} copy(f32[4,1,1024]{2,1,0:T(1,128)S(1)} %bitcast.18) | data formatting | bytes 32768
  53.8 0.6 %copy.21 = f32[4,1,1024]{2,1,0:T(1,128)} copy(f32[4,1,1024]{2,1,0:T(1,128)S(1)} %bitcast.17) | data formatting | bytes 32768
  54.4 0.6 %copy.22 = f32[4,1,1024]{2,1,0:T(1,128)} copy(f32[4,1,1024]{2,1,0:T(1,128)S(1)} %bitcast.16) | data formatting | bytes 32768
  (5 shorter events, 0.0 us)
Async XLA Ops:
  0.6 0.7 %copy-start.9 = (s32[4,1]{0,1:T(1,128)S(1)}, s32[4,1]{0,1:T(1,128)}, u32[]{:S(2)}) copy-start(s32[4,1]{0,1:T(1,128)} %param.10) | copy-start | bytes 52
  1.3 0.7 %copy-start.8 = (s32[4,1]{0,1:T(1,128)S(1)}, s32[4,1]{0,1:T(1,128)}, u32[]{:S(2)}) copy-start(s32[4,1]{0,1:T(1,128)} %param.13) | copy-start | bytes 52
  2.0 0.7 %copy-start = (f32[4,1,1024]{2,1,0:T(1,128)S(1)}, f32[4,1,1024]{2,1,0:T(1,128)}, u32[]{:S(2)}) copy-start(f32[4,1,1024]{2,1,0:T(1,128)} %param.11) | copy-start | bytes 49156
  2.8 0.7 %copy-start.2 = (f32[4,1,1024]{2,1,0:T(1,128)S(1)}, f32[4,1,1024]{2,1,0:T(1,128)}, u32[]{:S(2)}) copy-start(f32[4,1,1024]{2,1,0:T(1,128)} %param.16) | copy-start | bytes 49156
  3.5 0.8 %copy-start.4 = (f32[4,1,2,1024]{3,2,1,0:T(2,128)S(1)}, f32[4,1,2,1024]{3,2,1,0:T(2,128)}, u32[]{:S(2)}) copy-start(f32[4,1,2,1024]{3,2,1,0:T(2,128)} %param.9) | copy-start | bytes 98308
  16.6 20.8 %copy-start.1 = (f32[4,1,1024]{2,1,0:T(1,128)S(1)}, f32[4,1,1024]{2,1,0:T(1,128)}, u32[]{:S(2)}) copy-start(f32[4,1,1024]{2,1,0:T(1,128)} %param.11) | copy-start | bytes 49156
  16.6 20.8 %copy-start.3 = (f32[4,1,1024]{2,1,0:T(1,128)S(1)}, f32[4,1,1024]{2,1,0:T(1,128)}, u32[]{:S(2)}) copy-start(f32[4,1,1024]{2,1,0:T(1,128)} %param.16) | copy-start | bytes 49156
  16.6 20.8 %copy-start.5 = (f32[4,1,1024]{2,1,0:T(1,128)S(1)}, f32[4,1,1024]{2,1,0:T(1,128)}, u32[]{:S(2)}) copy-start(f32[4,1,1024]{2,1,0:T(1,128)} %param.12) | copy-start | bytes 49156
  16.6 20.7 %copy-start.6 = (f32[4,1,1024]{2,1,0:T(1,128)S(1)}, f32[4,1,1024]{2,1,0:T(1,128)}, u32[]{:S(2)}) copy-start(f32[4,1,1024]{2,1,0:T(1,128)} %param.15) | copy-start | bytes 49156
  16.6 20.7 %copy-start.7 = (f32[4,1,1024]{2,1,0:T(1,128)S(1)}, f32[4,1,1024]{2,1,0:T(1,128)}, u32[]{:S(2)}) copy-start(f32[4,1,1024]{2,1,0:T(1,128)} %param.14) | copy-start | bytes 49156
